TPU v7x, 256 devices: a whole 4x4x8 slice. The times are simulated.
256 devices in a mesh: leaf: 16 (over z, core), front: 16 (over x, y).
Axes of the slice: x: 4, y: 4, z: 8, core: 2. Of those that a mesh axis runs over, the one named last changes fastest.
Arguments:
- rhs_leaf: float32 [16, 1024, 256], P('leaf', 'front'), may hold values from -6 to 6
- rhs_top: float32 [15, 1024, 256], P(None, 'front'), may hold values from -6 to 6
- inv_leaf: bfloat16 [16, 1024, 1024], P('leaf', 'front'), as said below
- inv_top: bfloat16 [15, 1024, 1024], P(None, 'front'), as said below
- off_leaf: bfloat16 [16, 1024, 1024], P('leaf', None, 'front'), may hold values from -0.09375 to 0.09375
- off_top: bfloat16 [14, 1024, 1024], P(None, None, 'front'), may hold values from -0.09375 to 0.09375
- idx_leaf: int32 [16, 1024], P('leaf'), may hold values from 0 to 4095, as said below
- idx_top: int32 [14, 1024], replicated, may hold values from 0 to 3071, as said below
Outputs:
- leaf_solution: float32 [16, 1024, 256], P('leaf', 'front')
- ancestor_solution: float32 [16, 4, 1024, 256], P('leaf', None, 'front')
Inputs may be any that keep to these rules, and one draw needn't show every extreme that they name: `idx_leaf`: entry r of row g is a * 1024 + q with a < 4: update row r of split-level front g lands on row q of its depth-a ancestor. `idx_top`: row j belongs to the upper front with heap number h = j + 2; its entries are a * 1024 + q with a < floor(log2 h): update row r lands on row q of h's depth-a ancestor. `inv_leaf`: every block is lower triangular with a positive diagonal. `inv_top`: every block is lower triangular with a positive diagonal.
All inputs are finite; a program needn't handle non-finite values.
Results may differ from a plain program's by a relative error of at most 0.0055.
Values may be sent and summed in bfloat16 or wider, within the bound.
No kernel may reach another device: no remote copies, remote signals or barrier semaphores. Data moves between devices by JAX's collectives and lax.ppermute only.
A program may use at most 64 MiB of HBM per device.

v0:
```python
import jax
import jax.numpy as jnp
from jax import lax
from jax.sharding import PartitionSpec as P


def partner(block, axis, stride):
    count = lax.axis_size(axis)
    route = []
    for low in range(count):
        high = low | 1 << stride
        if high != low and high < count:
            route += [(low, high), (high, low)]
    return lax.ppermute(block, axis, route)


def local(rhs_leaf, rhs_top, inv_leaf, inv_top, off_leaf, off_top, idx_leaf, idx_top):
    front_width = inv_leaf.shape[2]
    rhs_count = rhs_leaf.shape[2]
    leaves = lax.axis_size("leaf")
    depth_count = leaves.bit_length() - 1
    leaf_pos = lax.axis_index("leaf")

    def apply_inverse(inverse, right_side):
        rounded = right_side.astype(jnp.bfloat16)
        return jnp.dot(
            inverse,
            lax.all_gather(rounded, "front", axis=0, tiled=True),
            preferred_element_type=jnp.float32,
        )

    def spread(off_block, solution, row_list, count):
        partial_value = jnp.dot(
            off_block, solution.astype(jnp.bfloat16), preferred_element_type=jnp.float32
        )
        dense_rows = jax.ops.segment_sum(partial_value, row_list, num_segments=count * front_width)
        dense_rows = dense_rows.reshape(count, front_width, rhs_count)
        return lax.psum_scatter(dense_rows, "front", scatter_dimension=1, tiled=True)

    leaf_solution = apply_inverse(inv_leaf[0], rhs_leaf[0])
    pending = spread(off_leaf[0], leaf_solution, idx_leaf[0], depth_count)
    solved = []
    for section_num in range(depth_count):
        pending = pending + partner(pending, "leaf", section_num)
        heap_node = jnp.right_shift(leaves + leaf_pos, section_num + 1)
        right_side = (
            lax.dynamic_index_in_dim(rhs_top, heap_node - 1, 0, keepdims=False) - pending[0]
        )
        inverse = lax.dynamic_index_in_dim(inv_top, heap_node - 1, 0, keepdims=False)
        solution = apply_inverse(inverse, right_side)
        solved.append(solution)
        if section_num + 1 < depth_count:
            off_block = lax.dynamic_index_in_dim(off_top, heap_node - 2, 0, keepdims=False)
            row_list = lax.dynamic_index_in_dim(idx_top, heap_node - 2, 0, keepdims=False)
            pending = pending[1:] + spread(
                off_block, solution, row_list, depth_count - section_num - 1
            )
    return (leaf_solution[None], jnp.stack(solved)[None])


def solution(mesh):
    placed = (
        P("leaf", "front", None),
        P(None, "front", None),
        P("leaf", "front", None),
        P(None, "front", None),
        P("leaf", None, "front"),
        P(None, None, "front"),
        P("leaf", None),
        P(),
    )
    return jax.shard_map(
        local,
        mesh=mesh,
        in_specs=placed,
        out_specs=(P("leaf", "front", None), P("leaf", None, "front", None)),
        check_vma=False,
    )
```

profile of v0, /device:TPU:32, one launch (start us, length us, event | category | flops | bytes accessed | tf_op | source)
XLA Modules:
  0.0 521.0 jit_solution(1386196292948095497)
XLA Ops:
  8.2 24.3 %all-gather = bf16[1,1024,256]{2,1,0:T(8,128)(2,1)S(1)} all-gather(bf16[1,64,256]{2,1,0:T(8,128)(2,1)S(1)} %convert_element_type.42), channel_id=2, replica_groups=mesh['leaf'=16,'front'=16] {'front'}, dimensions={1}, use_global_device_ids=true | all-gather | bytes 557056 | tf_op jit(solution)/shard_map/all_gather | solution.py:28
  32.5 1.1 fusion.13
  33.6 1.2 convolution_bitcast_fusion
  34.8 1.3 copy.10
  36.1 8.7 %scatter_custom_fusion = f32[4096,256]{1,0:T(8,128)} fusion(s32[1024]{0:T(1024)} %bitcast.71, f32[1024,256]{1,0:T(8,128)} %copy.10, f32[]{:T(128)} %constant.69.clone.1), kind=kCustom, calls=%fused_computation.4 | custom fusion | flops 262144 | bytes 4194816 | tf_op jit(solution)/shard_map/scatter-add | solution.py:36
  44.9 83.3 %reduce-scatter.5.cloned.1.call-done = f32[4,64,256]{2,1,0:T(8,128)} async-done(((f32[4,1024,256]{2,1,0:T(8,128)}), f32[4,64,256]{2,1,0:T(8,128)}) %reduce-scatter.5.cloned.1.call-update) | async-done | bytes 262160 | tf_op jit(solution)/shard_map/reduce_scatter | solution.py:38
  131.8 23.3 %all-gather.1 = bf16[1,1024,256]{2,1,0:T(8,128)(2,1)S(1)} all-gather(bf16[1,64,256]{2,1,0:T(8,128)(2,1)S(1)} %fusion.38), channel_id=3, replica_groups=mesh['leaf'=16,'front'=16] {'front'}, dimensions={1}, use_global_device_ids=true | all-gather | bytes 557056 | tf_op jit(solution)/shard_map/all_gather | solution.py:28
  155.2 1.2 fusion.23
  156.5 7.9 %scatter_custom_fusion.1 = f32[3072,256]{1,0:T(8,128)} fusion(s32[1024]{0:T(1024)S(1)} %bitcast.70, f32[1024,256]{1,0:T(8,128)S(1)} %fusion.23, f32[]{:T(128)} %constant.69.clone.1), kind=kCustom, calls=%fused_computation.6 | custom fusion | flops 262144 | bytes 3145732 | tf_op jit(solution)/shard_map/scatter-add | solution.py:36
  164.4 79.7 %reduce-scatter.7.cloned.1.call-done = f32[3,64,256]{2,1,0:T(8,128)} async-done(((f32[3,1024,256]{2,1,0:T(8,128)}), f32[3,64,256]{2,1,0:T(8,128)}) %reduce-scatter.7.cloned.1.call-update) | async-done | bytes 196624 | tf_op jit(solution)/shard_map/reduce_scatter | solution.py:38
  245.6 5.2 collective-permute-done.1
  251.7 23.5 %all-gather.2 = bf16[1,1024,256]{2,1,0:T(8,128)(2,1)S(1)} all-gather(bf16[1,64,256]{2,1,0:T(8,128)(2,1)S(1)} %fusion.37), channel_id=4, replica_groups=mesh['leaf'=16,'front'=16] {'front'}, dimensions={1}, use_global_device_ids=true | all-gather | bytes 557056 | tf_op jit(solution)/shard_map/all_gather | solution.py:28
  275.4 1.2 fusion.20
  276.7 7.5 %scatter_custom_fusion.2 = f32[2048,256]{1,0:T(8,128)} fusion(s32[1024]{0:T(1024)S(1)} %bitcast.69, f32[1024,256]{1,0:T(8,128)S(1)} %fusion.20, f32[]{:T(128)} %constant.69.clone.1), kind=kCustom, calls=%fused_computation.10 | custom fusion | flops 262144 | bytes 2097156 | tf_op jit(solution)/shard_map/scatter-add | solution.py:36
  284.2 78.2 %reduce-scatter.9.cloned.1.call-done = f32[2,64,256]{2,1,0:T(8,128)} async-done(((f32[2,1024,256]{2,1,0:T(8,128)}), f32[2,64,256]{2,1,0:T(8,128)}) %reduce-scatter.9.cloned.1.call-update) | async-done | bytes 131088 | tf_op jit(solution)/shard_map/reduce_scatter | solution.py:38
  363.3 2.6 collective-permute-start.2
  365.9 3.8 collective-permute-done.2
  370.6 23.2 %all-gather.3 = bf16[1,1024,256]{2,1,0:T(8,128)(2,1)S(1)} all-gather(bf16[1,64,256]{2,1,0:T(8,128)(2,1)S(1)} %fusion.36), channel_id=5, replica_groups=mesh['leaf'=16,'front'=16] {'front'}, dimensions={1}, use_global_device_ids=true | all-gather | bytes 557056 | tf_op jit(solution)/shard_map/all_gather | solution.py:28
  394.1 1.2 fusion.17
  395.3 7.1 %scatter_custom_fusion.3 = f32[1024,256]{1,0:T(8,128)} fusion(s32[1024]{0:T(1024)S(1)} %bitcast.68, f32[1024,256]{1,0:T(8,128)S(1)} %fusion.17, f32[]{:T(128)} %constant.69.clone.1), kind=kCustom, calls=%fused_computation.21 | custom fusion | flops 262144 | bytes 1048580 | tf_op jit(solution)/shard_map/scatter-add | solution.py:36
  402.4 77.7 %reduce-scatter.11.cloned.1.call-done = f32[1,64,256]{2,1,0:T(8,128)} async-done(((f32[1,1024,256]{2,1,0:T(8,128)}), f32[1,64,256]{2,1,0:T(8,128)}) %reduce-scatter.11.cloned.1.call-update) | async-done | bytes 65552 | tf_op jit(solution)/shard_map/reduce_scatter | solution.py:38
  480.9 5.0 collective-permute-start.3
  485.9 3.4 collective-permute-done.3
  490.2 23.3 %all-gather.4 = bf16[1,1024,256]{2,1,0:T(8,128)(2,1)S(1)} all-gather(bf16[1,64,256]{2,1,0:T(8,128)(2,1)S(1)} %subtract_convert_fusion), channel_id=6, replica_groups=mesh['leaf'=16,'front'=16] {'front'}, dimensions={1}, use_global_device_ids=true | all-gather | bytes 557056 | tf_op jit(solution)/shard_map/all_gather | solution.py:28
  (32 shorter events, 12.3 us)
Async XLA Ops:
  7.2 147.9 %copy-start = (bf16[15,64,1024]{2,1,0:T(8,128)(2,1)S(1)}, bf16[15,64,1024]{2,1,0:T(8,128)(2,1)}, u32[]{:S(2)}) copy-start(bf16[15,64,1024]{2,1,0:T(8,128)(2,1)} %param.11) | copy-start | bytes 5898244
  7.2 121.0 %reduce-scatter.5.cloned.1.call-start = ((), (), s32[]{:S(2)}) async-start(), calls=%async_computation.4 | async-start | bytes 4456448 | tf_op jit(solution)/shard_map/reduce_scatter | solution.py:38
  33.6 11.2 %copy-start.1 = (f32[64,256]{1,0:T(8,128)}, f32[64,256]{1,0:T(8,128)S(1)}, u32[]{:S(2)}) copy-start(f32[64,256]{1,0:T(8,128)S(1)} %fusion.13) | copy-start | bytes 196612
  44.8 199.3 %reduce-scatter.7.cloned.1.call-start = ((), (), s32[]{:S(2)}) async-start(), calls=%async_computation.5 | async-start | bytes 3342336 | tf_op jit(solution)/shard_map/reduce_scatter | solution.py:38
  128.2 1.7 collective-permute-start
  164.4 198.0 %reduce-scatter.9.cloned.1.call-start = ((), (), s32[]{:S(2)}) async-start(), calls=%async_computation.6 | async-start | bytes 2228224 | tf_op jit(solution)/shard_map/reduce_scatter | solution.py:38
  245.1 5.8 %collective-permute-start.1 = (f32[3,64,256]{2,1,0:T(8,128)S(1)}, f32[3,64,256]{2,1,0:T(8,128)S(1)}, u32[]{:S(2)}, u32[]{:S(2)}) collective-permute-start(f32[3,64,256]{2,1,0:T(8,128)S(1)} %slice_add_fusion), channel_id=1, source_target_pairs={{0,32},{32,0},{16,48},{48,16},{64,96},{96,64},{80,112},{112,80},{1... | collective-permute-start | bytes 589832 | tf_op jit(solution)/shard_map/ppermute | solution.py:14
  284.2 195.9 %reduce-scatter.11.cloned.1.call-start = ((), (), s32[]{:S(2)}) async-start(), calls=%async_computation.7 | async-start | bytes 1114112 | tf_op jit(solution)/shard_map/reduce_scatter | solution.py:38
  363.3 6.5 %collective-permute-start.2 = (f32[2,64,256]{2,1,0:T(8,128)S(1)}, f32[2,64,256]{2,1,0:T(8,128)S(1)}, u32[]{:S(2)}, u32[]{:S(2)}) collective-permute-start(f32[2,64,256]{2,1,0:T(8,128)S(1)} %slice_add_fusion.1), channel_id=1, source_target_pairs={{0,64},{64,0},{16,80},{80,16},{32,96},{96,32},{48,112},{112,48},{1... | collective-permute-start | bytes 393224 | tf_op jit(solution)/shard_map/ppermute | solution.py:14
  480.9 8.4 %collective-permute-start.3 = (f32[1,64,256]{2,1,0:T(8,128)S(1)}, f32[1,64,256]{2,1,0:T(8,128)S(1)}, u32[]{:S(2)}, u32[]{:S(2)}) collective-permute-start(f32[1,64,256]{2,1,0:T(8,128)S(1)} %slice_add_fusion.2), channel_id=1, source_target_pairs={{0,128},{128,0},{16,144},{144,16},{32,160},{160,32},{48,176},{176,... | collective-permute-start | bytes 196616 | tf_op jit(solution)/shard_map/ppermute | solution.py:14
Sparse Core Ops, SparseCore 0:
  45.0 83.1 reduce-scatter.4
  164.5 79.5 reduce-scatter.6
  284.3 78.0 reduce-scatter.8
  402.5 77.5 reduce-scatter.10
where the time goes:
time: 522 us; the launch traced here: 521 us
  waiting for transfers between devices  332 us (64%)
  blocking collectives  118 us (23%)
  other arithmetic  39.9 us (8%)
  between operations  13.9 us (3%)
  starting transfers between devices  8.32 us (2%)
  matrix products  6.91 us (1%)
    reduce_scatter x4, waiting for transfers between devices, spread(): lax.psum_scatter(dense_rows, 'front', scatter_dimension=1, tiled=True)  319 us
    all_gather x5, blocking collectives, apply_inverse(): lax.all_gather(rounded, 'front', axis=0, tiled=True)  118 us
    scatter-add x4, other arithmetic, spread(): jax.ops.segment_sum(partial_value, row_list, num_segments=count * front_w...  31.1 us
    ppermute x4, waiting for transfers between devices, partner(): return lax.ppermute(block, axis, route)  13.3 us
  transfers between devices with their start and end apart: 8, of which 8 were waited for; matrix products, arithmetic and copies ran while one was open for 0% of the time, Pallas kernels for 0%

commit v1 on v0

--- a/solution.py
+++ b/solution.py
@@ -25,7 +25,9 @@
         rounded = right_side.astype(jnp.bfloat16)
         return jnp.dot(
             inverse,
-            lax.all_gather(rounded, "front", axis=0, tiled=True),
+            jnp.concatenate(
+                lax.all_to_all(jnp.stack([rounded] * lax.axis_size("front")), "front", 0, 0), axis=0
+            ),
             preferred_element_type=jnp.float32,
         )
 

time: 522 us -> 480 us (0.920)
  blocking collectives: 118 us -> 62.6 us
  waiting for transfers between devices: 332 us -> 340 us
    all_gather x5 -> x0, blocking collectives: 118 us -> none  [apply_inverse(): lax.all_gather(rounded, 'front', axis=0, tiled=True)]
    all_to_all x0 -> x4, blocking collectives: none -> 62.6 us  [apply_inverse(): lax.all_to_all(jnp.stack([rounded] * lax.axis_size('front')), 'front', 0, 0)]
    all_to_all x0 -> x1, waiting for transfers between devices: none -> 10.8 us  [apply_inverse(): lax.all_to_all(jnp.stack([rounded] * lax.axis_size('front')), 'front', 0, 0)]
  transfers between devices with their start and end apart: 8 -> 9, of which waited for: 8 -> 9; matrix products, arithmetic and copies ran while one was open for 0% -> 0% of each run, Pallas kernels for 0% -> 0%
where the time goes in v1:
time: 480 us; the launch traced here: 479 us
  waiting for transfers between devices  340 us (71%)
  blocking collectives  62.6 us (13%)
  other arithmetic  39.9 us (8%)
  between operations  13.9 us (3%)
  starting transfers between devices  13.1 us (3%)
  matrix products  5.97 us (1%)
    reduce_scatter x4, waiting for transfers between devices, spread(): lax.psum_scatter(dense_rows, 'front', scatter_dimension=1, tiled=True)  315 us
    all_to_all x4, blocking collectives, apply_inverse(): lax.all_to_all(jnp.stack([rounded] * lax.axis_size('front')), 'front', 0, 0)  62.6 us
    scatter-add x4, other arithmetic, spread(): jax.ops.segment_sum(partial_value, row_list, num_segments=count * front_w...  31.1 us
    ppermute x4, waiting for transfers between devices, partner(): return lax.ppermute(block, axis, route)  14.2 us
    all_to_all x1, waiting for transfers between devices, apply_inverse(): lax.all_to_all(jnp.stack([rounded] * lax.axis_size('front')), 'front', 0, 0)  10.8 us
  transfers between devices with their start and end apart: 9, of which 9 were waited for; matrix products, arithmetic and copies ran while one was open for 0% of the time, Pallas kernels for 0%

profile of v1, /device:TPU:32, one launch (start us, length us, event | category | flops | bytes accessed | tf_op | source)
XLA Modules:
  0.0 479.2 jit_solution(2332712241670819883)
XLA Ops:
  8.3 18.3 %all_to_all.25 = bf16[16,64,256]{2,1,0:T(8,128)(2,1)S(1)} all-to-all(bf16[16,64,256]{2,1,0:T(8,128)(2,1)S(1)} %stack.31), channel_id=1, replica_groups=mesh['leaf'=16,'front'=16] {'front'}, dimensions={0} | all-to-all | bytes 1048576 | tf_op jit(solution)/shard_map/all_to_all | solution.py:29
  28.1 1.3 copy.10
  29.4 8.7 %scatter_custom_fusion = f32[4096,256]{1,0:T(8,128)} fusion(s32[1024]{0:T(1024)} %bitcast.81, f32[1024,256]{1,0:T(8,128)} %copy.10, f32[]{:T(128)} %constant.69.clone.1), kind=kCustom, calls=%fused_computation.4 | custom fusion | flops 262144 | bytes 4194816 | tf_op jit(solution)/shard_map/scatter-add | solution.py:38
  38.1 81.9 %reduce-scatter.5.cloned.1.call-done = f32[4,64,256]{2,1,0:T(8,128)} async-done(((f32[4,1024,256]{2,1,0:T(8,128)}), f32[4,64,256]{2,1,0:T(8,128)}) %reduce-scatter.5.cloned.1.call-update) | async-done | bytes 262160 | tf_op jit(solution)/shard_map/reduce_scatter | solution.py:40
  120.0 1.7 collective-permute-done
  124.4 4.9 %all-to-all-start.1 = ((bf16[16,64,256]{2,1,0:T(8,128)(2,1)}), bf16[16,64,256]{2,1,0:T(8,128)(2,1)S(1)}, u32[]{:S(2)}, u32[]{:S(2)}) async-start(bf16[16,64,256]{2,1,0:T(8,128)(2,1)} %stack.33), calls=%async_computation.2 | async-start | bytes 1048576 | tf_op jit(solution)/shard_map/all_to_all | solution.py:29
  130.3 10.8 %all-to-all-done.1 = bf16[16,64,256]{2,1,0:T(8,128)(2,1)S(1)} async-done(((bf16[16,64,256]{2,1,0:T(8,128)(2,1)}), bf16[16,64,256]{2,1,0:T(8,128)(2,1)S(1)}, u32[]{:S(2)}, u32[]{:S(2)}) %all-to-all-start.1) | async-done | bytes 524320 | tf_op jit(solution)/shard_map/all_to_all | solution.py:29
  141.3 1.2 fusion.15
  142.6 7.9 %scatter_custom_fusion.1 = f32[3072,256]{1,0:T(8,128)} fusion(s32[1024]{0:T(1024)S(1)} %bitcast.80, f32[1024,256]{1,0:T(8,128)S(1)} %fusion.15, f32[]{:T(128)} %constant.69.clone.1), kind=kCustom, calls=%fused_computation.6 | custom fusion | flops 262144 | bytes 3145732 | tf_op jit(solution)/shard_map/scatter-add | solution.py:38
  150.5 78.9 %reduce-scatter.7.cloned.1.call-done = f32[3,64,256]{2,1,0:T(8,128)} async-done(((f32[3,1024,256]{2,1,0:T(8,128)}), f32[3,64,256]{2,1,0:T(8,128)}) %reduce-scatter.7.cloned.1.call-update) | async-done | bytes 196624 | tf_op jit(solution)/shard_map/reduce_scatter | solution.py:40
  231.0 5.2 %collective-permute-done.1 = f32[3,64,256]{2,1,0:T(8,128)S(1)} collective-permute-done((f32[3,64,256]{2,1,0:T(8,128)S(1)}, f32[3,64,256]{2,1,0:T(8,128)S(1)}, u32[]{:S(2)}, u32[]{:S(2)}) %collective-permute-start.1) | collective-permute-done | bytes 196640 | tf_op jit(solution)/shard_map/ppermute | solution.py:14
  237.1 14.7 %all_to_all.26 = bf16[16,64,256]{2,1,0:T(8,128)(2,1)S(1)} all-to-all(bf16[16,64,256]{2,1,0:T(8,128)(2,1)S(1)} %stack.36), channel_id=1, replica_groups=mesh['leaf'=16,'front'=16] {'front'}, dimensions={0} | all-to-all | bytes 1048576 | tf_op jit(solution)/shard_map/all_to_all | solution.py:29
  252.1 1.2 fusion.11
  253.3 7.5 %scatter_custom_fusion.2 = f32[2048,256]{1,0:T(8,128)} fusion(s32[1024]{0:T(1024)S(1)} %bitcast.79, f32[1024,256]{1,0:T(8,128)S(1)} %fusion.11, f32[]{:T(128)} %constant.69.clone.1), kind=kCustom, calls=%fused_computation.10 | custom fusion | flops 262144 | bytes 2097156 | tf_op jit(solution)/shard_map/scatter-add | solution.py:38
  260.9 77.4 %reduce-scatter.9.cloned.1.call-done = f32[2,64,256]{2,1,0:T(8,128)} async-done(((f32[2,1024,256]{2,1,0:T(8,128)}), f32[2,64,256]{2,1,0:T(8,128)}) %reduce-scatter.9.cloned.1.call-update) | async-done | bytes 131088 | tf_op jit(solution)/shard_map/reduce_scatter | solution.py:40
  339.2 2.6 collective-permute-start.2
  341.8 3.8 collective-permute-done.2
  346.6 14.7 %all_to_all.27 = bf16[16,64,256]{2,1,0:T(8,128)(2,1)S(1)} all-to-all(bf16[16,64,256]{2,1,0:T(8,128)(2,1)S(1)} %stack.39), channel_id=1, replica_groups=mesh['leaf'=16,'front'=16] {'front'}, dimensions={0} | all-to-all | bytes 1048576 | tf_op jit(solution)/shard_map/all_to_all | solution.py:29
  361.5 1.2 fusion.8
  362.7 7.1 %scatter_custom_fusion.3 = f32[1024,256]{1,0:T(8,128)} fusion(s32[1024]{0:T(1024)S(1)} %bitcast.78, f32[1024,256]{1,0:T(8,128)S(1)} %fusion.8, f32[]{:T(128)} %constant.69.clone.1), kind=kCustom, calls=%fused_computation.12 | custom fusion | flops 262144 | bytes 1048580 | tf_op jit(solution)/shard_map/scatter-add | solution.py:38
  369.8 76.9 %reduce-scatter.11.cloned.1.call-done = f32[1,64,256]{2,1,0:T(8,128)} async-done(((f32[1,1024,256]{2,1,0:T(8,128)}), f32[1,64,256]{2,1,0:T(8,128)}) %reduce-scatter.11.cloned.1.call-update) | async-done | bytes 65552 | tf_op jit(solution)/shard_map/reduce_scatter | solution.py:40
  447.6 4.9 %collective-permute-start.3 = (f32[1,64,256]{2,1,0:T(8,128)S(1)}, f32[1,64,256]{2,1,0:T(8,128)S(1)}, u32[]{:S(2)}, u32[]{:S(2)}) collective-permute-start(f32[1,64,256]{2,1,0:T(8,128)S(1)} %slice_add_fusion.2), channel_id=1, source_target_pairs={{0,128},{128,0},{16,144},{144,16},{32,160},{160,32},{48,176},{176,... | collective-permute-start | bytes 196616 | tf_op jit(solution)/shard_map/ppermute | solution.py:14
  452.5 3.5 collective-permute-done.3
  456.9 14.8 %all_to_all.28 = bf16[16,64,256]{2,1,0:T(8,128)(2,1)S(1)} all-to-all(bf16[16,64,256]{2,1,0:T(8,128)(2,1)S(1)} %stack.42), channel_id=1, replica_groups=mesh['leaf'=16,'front'=16] {'front'}, dimensions={0} | all-to-all | bytes 1048576 | tf_op jit(solution)/shard_map/all_to_all | solution.py:29
  (40 shorter events, 13.8 us)
Async XLA Ops:
  7.2 134.0 %copy-start = (bf16[15,64,1024]{2,1,0:T(8,128)(2,1)S(1)}, bf16[15,64,1024]{2,1,0:T(8,128)(2,1)}, u32[]{:S(2)}) copy-start(bf16[15,64,1024]{2,1,0:T(8,128)(2,1)} %param.11) | copy-start | bytes 5898244
  7.2 20.5 %copy-start.2 = (bf16[1,1024,64]{1,2,0:T(8,128)(2,1)S(1)}, bf16[1,1024,64]{1,2,0:T(8,128)(2,1)}, u32[]{:S(2)}) copy-start(bf16[1,1024,64]{1,2,0:T(8,128)(2,1)} %param.12) | copy-start | bytes 393220
  7.2 112.8 %reduce-scatter.5.cloned.1.call-start = ((), (), s32[]{:S(2)}) async-start(), calls=%async_computation.9 | async-start | bytes 4456448 | tf_op jit(solution)/shard_map/reduce_scatter | solution.py:40
  27.7 10.3 %copy-start.1 = (f32[64,256]{1,0:T(8,128)}, f32[64,256]{1,0:T(8,128)S(1)}, u32[]{:S(2)}) copy-start(f32[64,256]{1,0:T(8,128)S(1)} %fusion.22) | copy-start | bytes 196612
  120.0 1.7 collective-permute-start
  124.4 16.7 %all-to-all-start.1 = ((bf16[16,64,256]{2,1,0:T(8,128)(2,1)}), bf16[16,64,256]{2,1,0:T(8,128)(2,1)S(1)}, u32[]{:S(2)}, u32[]{:S(2)}) async-start(bf16[16,64,256]{2,1,0:T(8,128)(2,1)} %stack.33), calls=%async_computation.2 | async-start | bytes 1048576 | tf_op jit(solution)/shard_map/all_to_all | solution.py:29
  129.3 100.1 %reduce-scatter.7.cloned.1.call-start = ((), (), s32[]{:S(2)}) async-start(), calls=%async_computation.10 | async-start | bytes 3342336 | tf_op jit(solution)/shard_map/reduce_scatter | solution.py:40
  150.5 187.8 %reduce-scatter.9.cloned.1.call-start = ((), (), s32[]{:S(2)}) async-start(), calls=%async_computation.11 | async-start | bytes 2228224 | tf_op jit(solution)/shard_map/reduce_scatter | solution.py:40
  230.4 5.8 %collective-permute-start.1 = (f32[3,64,256]{2,1,0:T(8,128)S(1)}, f32[3,64,256]{2,1,0:T(8,128)S(1)}, u32[]{:S(2)}, u32[]{:S(2)}) collective-permute-start(f32[3,64,256]{2,1,0:T(8,128)S(1)} %slice_add_fusion), channel_id=1, source_target_pairs={{0,32},{32,0},{16,48},{48,16},{64,96},{96,64},{80,112},{112,80},{1... | collective-permute-start | bytes 589832 | tf_op jit(solution)/shard_map/ppermute | solution.py:14
  260.8 185.9 %reduce-scatter.11.cloned.1.call-start = ((), (), s32[]{:S(2)}) async-start(), calls=%async_computation.12 | async-start | bytes 1114112 | tf_op jit(solution)/shard_map/reduce_scatter | solution.py:40
  339.2 6.4 %collective-permute-start.2 = (f32[2,64,256]{2,1,0:T(8,128)S(1)}, f32[2,64,256]{2,1,0:T(8,128)S(1)}, u32[]{:S(2)}, u32[]{:S(2)}) collective-permute-start(f32[2,64,256]{2,1,0:T(8,128)S(1)} %slice_add_fusion.1), channel_id=1, source_target_pairs={{0,64},{64,0},{16,80},{80,16},{32,96},{96,32},{48,112},{112,48},{1... | collective-permute-start | bytes 393224 | tf_op jit(solution)/shard_map/ppermute | solution.py:14
  447.6 8.4 %collective-permute-start.3 = (f32[1,64,256]{2,1,0:T(8,128)S(1)}, f32[1,64,256]{2,1,0:T(8,128)S(1)}, u32[]{:S(2)}, u32[]{:S(2)}) collective-permute-start(f32[1,64,256]{2,1,0:T(8,128)S(1)} %slice_add_fusion.2), channel_id=1, source_target_pairs={{0,128},{128,0},{16,144},{144,16},{32,160},{160,32},{48,176},{176,... | collective-permute-start | bytes 196616 | tf_op jit(solution)/shard_map/ppermute | solution.py:14
Sparse Core Ops, SparseCore 0:
  38.2 81.7 reduce-scatter.4
  150.6 78.8 reduce-scatter.6
  260.9 77.2 reduce-scatter.8
  369.9 76.7 reduce-scatter.10
